TPU v7x, 256 devices: a whole 4x4x8 slice. The times are simulated.
256 devices in a mesh: subj: 16 (over z_lo, x, core), space: 16 (over z_hi, y).
Axes of the slice: x: 4, y: 4, z: 8 (z_hi: 4, z_lo: 2; z = z_hi * 2 + z_lo), core: 2. Of those that a mesh axis runs over, the one named last changes fastest.
Arguments:
- image: bfloat16 [32, 16, 24, 48, 128], P('subj', 'space'), may hold values from -6 to 6
- momentum: bfloat16 [32, 3, 16, 24, 48, 128], P('subj', None, 'space'), may hold values from -128 to 128
- tissue_flags: int32 [32, 16], P('subj', 'space'), may hold values 0 or 1
- band_widths: int32 [3], replicated, may hold values from 8 to 12, as said below
Outputs:
- mismatch: bfloat16 [32, 16, 24, 48, 128], P('subj', 'space')
- template: float32 [16, 24, 48, 128], P('space')
Inputs may be any that keep to these rules, and one draw needn't show every extreme that they name: `band_widths`: the three widths are 8, 10 and 12 in some order.
All inputs are finite; a program needn't handle non-finite values. No bound on the sum of `tissue_flags` on one device may be relied on, other than what follows from the above.
Results may differ from a plain program's by a relative error of at most 0.001.
Values sent between devices are 32-bit elements; how exact they have to be, the bound alone decides.
A program may use at most 64 MiB of HBM per device.

v0:
```python
import jax
import jax.numpy as jnp
from jax import lax
from jax.sharding import PartitionSpec as P

TGY = 4
HALO = 12
STEPS = 4


def shifted(shard, axis, by):
    count = lax.axis_size(axis)
    pairs = [(i, i + by) for i in range(count) if 0 <= i + by < count]
    return lax.ppermute(shard, axis, pairs)


def extend(field, wide_x, wide_y):
    place = lax.axis_index("space")
    column = place % TGY
    if wide_x > 0:
        north = shifted(field[..., -wide_x:, :, :], "space", TGY)
        south = shifted(field[..., :wide_x, :, :], "space", -TGY)
        field = jnp.concatenate([north, field, south], axis=-3)
    if wide_y > 0:
        west = shifted(field[..., :, -wide_y:, :], "space", 1)
        east = shifted(field[..., :, :wide_y, :], "space", -1)
        west = jnp.where(column > 0, west, 0.0)
        east = jnp.where(column < TGY - 1, east, 0.0)
        field = jnp.concatenate([west, field, east], axis=-2)
    return field


def band_matrix(rows, cols, offset, width):
    row_ids = jnp.arange(rows)[:, None]
    col_ids = jnp.arange(cols)[None, :]
    dist = jnp.abs(col_ids - offset - row_ids).astype(jnp.float32)
    return jnp.where(dist <= width, (width + 1.0 - dist) / ((width + 1.0) * (width + 1.0)), 0.0)


def smooth_first(field, width):
    count = field.shape[-3]
    matrix = band_matrix(count - 2 * HALO, count, HALO, width)
    return jnp.einsum("ij,abjyz->abiyz", matrix, field, precision=lax.Precision.HIGHEST)


def smooth_second(field, width):
    count = field.shape[-2]
    matrix = band_matrix(count - 2 * HALO, count, HALO, width)
    return jnp.einsum("ij,abxjz->abxiz", matrix, field, precision=lax.Precision.HIGHEST)


def smooth_third(field, width):
    count = field.shape[-1]
    matrix = band_matrix(count, count, 0, width)
    return jnp.einsum("abxyz,wz->abxyw", field, matrix, precision=lax.Precision.HIGHEST)


def depth_pair(field):
    padded = jnp.pad(field, ((0, 0), (0, 0), (0, 0), (1, 1)))
    return (padded[..., :-2], padded[..., 2:])


def advance(padded, speed):
    centre = padded[:, 1:-1, 1:-1, :]
    pairs = (
        (padded[:, :-2, 1:-1, :], padded[:, 2:, 1:-1, :]),
        (padded[:, 1:-1, :-2, :], padded[:, 1:-1, 2:, :]),
        depth_pair(centre),
    )
    flux = jnp.zeros_like(centre)
    for axis in range(3):
        lower, upper = pairs[axis]
        rate = speed[:, axis]
        flux = (
            flux
            + jnp.maximum(rate, 0.0) * (centre - lower)
            + jnp.minimum(rate, 0.0) * (upper - centre)
        )
    return centre - 1.0 / STEPS * flux


def per_device(image, momentum, tissue_flags, band_widths):
    widths = band_widths.astype(jnp.float32)
    volume = image[:, 0].astype(jnp.float32)
    moment = momentum[:, :, 0].astype(jnp.float32)
    velocity = smooth_first(extend(moment, HALO, 0), widths[0])
    velocity = smooth_second(extend(velocity, 0, HALO), widths[1])
    velocity = smooth_third(velocity, widths[2])
    padded_velocity = extend(velocity, 1, 1)
    warped = volume
    for step in range(STEPS):
        warped = advance(extend(warped, 1, 1), velocity)
    grad_x = 0.5 * (padded_velocity[:, 0, 2:, 1:-1, :] - padded_velocity[:, 0, :-2, 1:-1, :])
    grad_y = 0.5 * (padded_velocity[:, 1, 1:-1, 2:, :] - padded_velocity[:, 1, 1:-1, :-2, :])
    lower_z, upper_z = depth_pair(padded_velocity[:, 2, 1:-1, 1:-1, :])
    divergence = grad_x + grad_y + 0.5 * (upper_z - lower_z)
    flags = tissue_flags[:, 0].astype(jnp.float32)[:, None, None, None]
    weight = flags * jnp.exp(divergence)
    numer = jnp.sum(weight * warped, axis=0)
    denom = jnp.sum(weight, axis=0)
    numer_all, denom_all = lax.psum((numer, denom), "subj")
    template = numer_all / (1.0 + denom_all)
    mismatch = (warped - template[None]).astype(jnp.bfloat16)
    return (mismatch[:, None], template[None])


def solution(mesh):
    return jax.shard_map(
        per_device,
        mesh=mesh,
        in_specs=(
            P("subj", "space", None, None, None),
            P("subj", None, "space", None, None, None),
            P("subj", "space"),
            P(),
        ),
        out_specs=(P("subj", "space", None, None, None), P("space", None, None, None)),
        check_vma=False,
    )
```

profile of v0, /device:TPU:1, one launch (start us, length us, event | category | flops | bytes accessed | tf_op | source)
XLA Modules:
  0.0 406.5 jit_solution(13739261991376798124)
XLA Ops:
  7.2 0.0 all-reduce.8.cloned.1.call-start
  7.2 1.8 bitcast_convert_fusion
  9.0 0.4 fusion.143
  9.5 1.8 copy.14
  11.3 6.9 %collective-permute-start = (f32[2,3,12,48,128]{4,3,2,1,0:T(8,128)}, f32[2,3,12,48,128]{4,3,2,1,0:T(8,128)}, u32[]{:S(2)}, u32[]{:S(2)}) collective-permute-start(f32[2,3,12,48,128]{4,3,2,1,0:T(8,128)} %copy.14), channel_id=1, source_target_pairs={{0,4},{1,5},{2,6},{3,7},{4,8},{5,9},{6,10},{7,11},{8,12},{9,13},{1... | collective-permute-start | bytes 5308424 | tf_op jit(solution)/shard_map/ppermute | solution.py:14
  18.2 1.8 copy.15
  20.0 1.3 collective-permute-start.1
  21.3 0.7 fusion.148
  22.6 1.1 bitcast_convert_fusion.1
  23.8 30.8 %collective-permute-done = f32[2,3,12,48,128]{4,3,2,1,0:T(8,128)} collective-permute-done((f32[2,3,12,48,128]{4,3,2,1,0:T(8,128)}, f32[2,3,12,48,128]{4,3,2,1,0:T(8,128)}, u32[]{:S(2)}, u32[]{:S(2)}) %collective-permute-start) | collective-permute-done | bytes 1769504 | tf_op jit(solution)/shard_map/ppermute | solution.py:14
  54.6 2.0 copy.16
  56.7 44.8 %collective-permute-done.1 = f32[2,3,12,48,128]{4,3,2,1,0:T(8,128)} collective-permute-done((f32[2,3,12,48,128]{4,3,2,1,0:T(8,128)}, f32[2,3,12,48,128]{4,3,2,1,0:T(8,128)}, u32[]{:S(2)}, u32[]{:S(2)}) %collective-permute-start.1) | collective-permute-done | bytes 1769504 | tf_op jit(solution)/shard_map/ppermute | solution.py:14
  101.5 2.0 copy.17
  103.5 5.5 %fusion.10 = f32[2,3,24,48,128]{4,2,3,1,0:T(8,128)S(1)} fusion(f32[2,3,12,48,128]{4,2,3,1,0:T(8,128)S(1)} %copy.17, f32[2,3,24,48,128]{4,2,3,1,0:T(8,128)S(1)} %bitcast_convert_fusion, f32[2,3,12,48,128]{4,2,3,1,0:T(8,128)S(1)} %copy.16, f32[]{:T(128)S(6)} %mul.111, f32[]{:T(128)S(6)} %add.126, f32[]{:T(128)} %bitcast.4, s32[48]{0:T(128)S(1)} %iota_add_fusion.1), kind=kOutput, calls=%fused_computation.28 | convolution fusion | flops 513154944 | bytes 10617036 | tf_op jit(solution)/shard_map/ij,abjyz->abiyz/dot_general | solution.py:43
  109.0 0.1 fusion.142
  109.1 1.6 copy-done
  110.7 3.2 collective-permute-start.2
  114.0 5.5 %collective-permute-start.4 = (f32[2,1,48,128]{3,2,1,0:T(8,128)S(1)}, f32[2,1,48,128]{3,2,1,0:T(8,128)S(1)}, u32[]{:S(2)}, u32[]{:S(2)}) collective-permute-start(f32[2,1,48,128]{3,2,1,0:T(8,128)S(1)} %get-tuple-element.33), channel_id=1, source_target_pairs={{0,4},{1,5},{2,6},{3,7},{4,8},{5,9},{6,10},{7,11},{8,12},{9,13},{1... | collective-permute-start | bytes 147464 | tf_op jit(solution)/shard_map/ppermute | solution.py:14
  119.5 1.3 collective-permute-start.5
  120.8 1.3 collective-permute-start.3
  122.1 4.3 %collective-permute-done.5 = f32[2,1,48,128]{3,2,1,0:T(8,128)S(1)} collective-permute-done((f32[2,1,48,128]{3,2,1,0:T(8,128)S(1)}, f32[2,1,48,128]{3,2,1,0:T(8,128)S(1)}, u32[]{:S(2)}, u32[]{:S(2)}) %collective-permute-start.5) | collective-permute-done | bytes 49184 | tf_op jit(solution)/shard_map/ppermute | solution.py:14
  126.5 0.7 pad_maximum_fusion.55
  127.1 2.6 collective-permute-start.6
  131.1 1.5 collective-permute-start.7
  132.6 10.3 %collective-permute-done.7 = f32[2,26,1,128]{3,2,1,0:T(1,128)S(1)} collective-permute-done((f32[2,26,1,128]{3,2,1,0:T(1,128)}, f32[2,26,1,128]{3,2,1,0:T(1,128)S(1)}, u32[]{:S(2)}, u32[]{:S(2)}) %collective-permute-start.7) | collective-permute-done | bytes 26656 | tf_op jit(solution)/shard_map/ppermute | solution.py:14
  142.9 0.1 broadcast_select_fusion.1
  143.0 0.1 broadcast_select_fusion
  143.1 1.8 copy-done.1
  144.9 0.3 pad_maximum_fusion
  145.3 5.3 %fusion.6 = f32[2,3,24,128,48]{3,4,2,1,0:T(8,128)S(1)} fusion(f32[2,3,24,72,128]{4,2,3,1,0:T(8,128)S(1)} %pad_maximum_fusion, f32[]{:T(128)S(6)} %mul.112, f32[]{:T(128)S(6)} %add.127, f32[]{:T(128)} %bitcast.8, s32[72]{0:T(128)S(1)} %iota_add_fusion), kind=kOutput, calls=%fused_computation.7 | convolution fusion | flops 764436096 | bytes 8847660 | tf_op jit(solution)/shard_map/ij,abxjz->abxiz/dot_general | solution.py:49
  150.6 3.8 fusion.8
  154.5 1.6 convert_subtract_fusion
  156.1 22.1 %collective-permute-start.8 = (f32[2,1,48,128]{3,2,1,0:T(8,128)S(1)}, f32[2,1,48,128]{3,2,1,0:T(8,128)S(1)}, u32[]{:S(2)}, u32[]{:S(2)}) collective-permute-start(f32[2,1,48,128]{3,2,1,0:T(8,128)S(1)} %get-tuple-element.31), channel_id=1, source_target_pairs={{0,4},{1,5},{2,6},{3,7},{4,8},{5,9},{6,10},{7,11},{8,12},{9,13},{1... | collective-permute-start | bytes 147464 | tf_op jit(solution)/shard_map/ppermute | solution.py:14
  178.1 1.3 collective-permute-start.9
  179.5 5.9 %collective-permute-done.9 = f32[2,1,48,128]{3,2,1,0:T(8,128)S(1)} collective-permute-done((f32[2,1,48,128]{3,2,1,0:T(8,128)S(1)}, f32[2,1,48,128]{3,2,1,0:T(8,128)S(1)}, u32[]{:S(2)}, u32[]{:S(2)}) %collective-permute-start.9) | collective-permute-done | bytes 49184 | tf_op jit(solution)/shard_map/ppermute | solution.py:14
  185.4 1.3 collective-permute-start.10
  186.7 1.3 collective-permute-start.11
  188.1 3.2 collective-permute-done.11
  191.3 1.5 fusion.30
  192.9 8.8 %collective-permute-start.12 = (f32[2,1,48,128]{3,2,1,0:T(8,128)S(1)}, f32[2,1,48,128]{3,2,1,0:T(8,128)S(1)}, u32[]{:S(2)}, u32[]{:S(2)}) collective-permute-start(f32[2,1,48,128]{3,2,1,0:T(8,128)S(1)} %get-tuple-element.29), channel_id=1, source_target_pairs={{0,4},{1,5},{2,6},{3,7},{4,8},{5,9},{6,10},{7,11},{8,12},{9,13},{1... | collective-permute-start | bytes 147464 | tf_op jit(solution)/shard_map/ppermute | solution.py:14
  201.7 1.3 collective-permute-start.13
  203.0 0.1 slice_bitcast_fusion
  203.1 5.1 %collective-permute-done.13 = f32[2,1,48,128]{3,2,1,0:T(8,128)S(1)} collective-permute-done((f32[2,1,48,128]{3,2,1,0:T(8,128)S(1)}, f32[2,1,48,128]{3,2,1,0:T(8,128)S(1)}, u32[]{:S(2)}, u32[]{:S(2)}) %collective-permute-start.13) | collective-permute-done | bytes 49184 | tf_op jit(solution)/shard_map/ppermute | solution.py:14
  208.3 2.1 collective-permute-start.14
  210.4 1.3 collective-permute-start.20
  211.7 5.9 %collective-permute-start.21 = (f32[2,3,1,48,128]{4,3,2,1,0:T(8,128)S(1)}, f32[2,3,1,48,128]{4,3,2,1,0:T(8,128)S(1)}, u32[]{:S(2)}, u32[]{:S(2)}) collective-permute-start(f32[2,3,1,48,128]{4,3,2,1,0:T(8,128)S(1)} %get-tuple-element.13), channel_id=1, source_target_pairs={{0,4},{1,5},{2,6},{3,7},{4,8},{5,9},{6,10},{7,11},{8,12},{9,13},{1... | collective-permute-start | bytes 442376 | tf_op jit(solution)/shard_map/ppermute | solution.py:14
  217.6 1.3 collective-permute-start.15
  219.0 3.5 collective-permute-done.15
  222.6 1.5 fusion.38
  224.1 7.2 %collective-permute-start.16 = (f32[2,1,48,128]{3,2,1,0:T(8,128)S(1)}, f32[2,1,48,128]{3,2,1,0:T(8,128)S(1)}, u32[]{:S(2)}, u32[]{:S(2)}) collective-permute-start(f32[2,1,48,128]{3,2,1,0:T(8,128)S(1)} %get-tuple-element.27), channel_id=1, source_target_pairs={{0,4},{1,5},{2,6},{3,7},{4,8},{5,9},{6,10},{7,11},{8,12},{9,13},{1... | collective-permute-start | bytes 147464 | tf_op jit(solution)/shard_map/ppermute | solution.py:14
  231.3 1.3 collective-permute-start.17
  232.7 0.1 pad_maximum_fusion.43
  232.8 1.3 collective-permute-start.22
  234.1 4.0 collective-permute-start.23
  238.1 2.2 collective-permute-start.18
  240.4 1.3 collective-permute-start.19
  241.7 0.1 broadcast_select_fusion.3
  241.8 0.1 broadcast_select_fusion.2
  241.9 7.1 %collective-permute-done.19 = f32[2,26,1,128]{3,2,1,0:T(1,128)S(1)} collective-permute-done((f32[2,26,1,128]{3,2,1,0:T(1,128)S(1)}, f32[2,26,1,128]{3,2,1,0:T(1,128)S(1)}, u32[]{:S(2)}, u32[]{:S(2)}) %collective-permute-start.19) | collective-permute-done | bytes 26656 | tf_op jit(solution)/shard_map/ppermute | solution.py:14
  249.0 5.2 %fusion.139 = (f32[24,48,128]{2,1,0:T(8,128)}, f32[24,48,128]{2,1,0:T(8,128)}, f32[2,24,48,128]{3,2,1,0:T(8,128)S(1)}) fusion(f32[2,24,48,128]{3,2,1,0:T(8,128)S(1)} %fusion.38, f32[2,3,24,48,128]{4,3,2,1,0:T(8,128)S(1)} %fusion.8, f32[2,26,1,128]{3,2,1,0:T(1,128)S(1)} %broadcast_select_fusion.4, f32[2,1,48,128]{3,2,1,0:T(8,128)S(1)} %collective-permute-done.17, ...), kind=kLoop, calls=%fused_computation.236 | loop fusion | flops 14745600 | bytes 12403200 | tf_op jit(solution)/shard_map/reduce_sum | solution.py:100
  254.3 0.0 all-reduce.8.cloned.1.call-update
  254.3 143.0 %all-reduce.8.cloned.1.call-done = (f32[24,48,128]{2,1,0:T(8,128)}, f32[24,48,128]{2,1,0:T(8,128)}) async-done(((f32[24,48,128]{2,1,0:T(8,128)}, f32[24,48,128]{2,1,0:T(8,128)}), (f32[24,48,128]{2,1,0:T(8,128)}, f32[24,48,128]{2,1,0:T(8,128)})) %all-reduce.8.cloned.1.call-update) | async-done | bytes 1179664 | tf_op jit(solution)/shard_map/psum | solution.py:101
  397.3 1.3 add_divide_fusion
  398.6 1.0 fusion.95
  (57 shorter events, 0.5 us)
Async XLA Ops:
  7.2 390.1 %all-reduce.8.cloned.1.call-start = ((), (), s32[]{:S(2)}) async-start(), calls=%async_computation | async-start | bytes 2359296 | tf_op jit(solution)/shard_map/psum | solution.py:101
  11.3 43.3 %collective-permute-start = (f32[2,3,12,48,128]{4,3,2,1,0:T(8,128)}, f32[2,3,12,48,128]{4,3,2,1,0:T(8,128)}, u32[]{:S(2)}, u32[]{:S(2)}) collective-permute-start(f32[2,3,12,48,128]{4,3,2,1,0:T(8,128)} %copy.14), channel_id=1, source_target_pairs={{0,4},{1,5},{2,6},{3,7},{4,8},{5,9},{6,10},{7,11},{8,12},{9,13},{1... | collective-permute-start | bytes 5308424 | tf_op jit(solution)/shard_map/ppermute | solution.py:14
  18.2 3.1 copy-start.10
  20.0 81.4 %collective-permute-start.1 = (f32[2,3,12,48,128]{4,3,2,1,0:T(8,128)}, f32[2,3,12,48,128]{4,3,2,1,0:T(8,128)}, u32[]{:S(2)}, u32[]{:S(2)}) collective-permute-start(f32[2,3,12,48,128]{4,3,2,1,0:T(8,128)} %copy.15), channel_id=1, source_target_pairs={{4,0},{5,1},{6,2},{7,3},{8,4},{9,5},{10,6},{11,7},{12,8},{13,9},{1... | collective-permute-start | bytes 5308424 | tf_op jit(solution)/shard_map/ppermute | solution.py:14
  23.8 102.7 %copy-start.2 = (f32[2,24,48,128]{3,2,1,0:T(8,128)}, f32[2,24,48,128]{3,2,1,0:T(8,128)S(1)}, u32[]{:S(2)}) copy-start(f32[2,24,48,128]{3,2,1,0:T(8,128)S(1)} %bitcast_convert_fusion.1) | copy-start | bytes 3538948
  109.0 1.7 copy-start
  110.7 32.1 %collective-permute-start.2 = (f32[2,3,24,12,128]{4,2,3,1,0:T(8,128)S(1)}, f32[2,3,24,12,128]{4,2,3,1,0:T(8,128)S(1)}, u32[]{:S(2)}, u32[]{:S(2)}) collective-permute-start(f32[2,3,24,12,128]{4,2,3,1,0:T(8,128)S(1)} %get-tuple-element.15), channel_id=1, source_target_pairs={{0,1},{1,2},{2,3},{3,4},{4,5},{5,6},{6,7},{7,8},{8,9},{9,10},{10,1... | collective-permute-start | bytes 2654216 | tf_op jit(solution)/shard_map/ppermute | solution.py:14
  114.0 8.1 %collective-permute-start.4 = (f32[2,1,48,128]{3,2,1,0:T(8,128)S(1)}, f32[2,1,48,128]{3,2,1,0:T(8,128)S(1)}, u32[]{:S(2)}, u32[]{:S(2)}) collective-permute-start(f32[2,1,48,128]{3,2,1,0:T(8,128)S(1)} %get-tuple-element.33), channel_id=1, source_target_pairs={{0,4},{1,5},{2,6},{3,7},{4,8},{5,9},{6,10},{7,11},{8,12},{9,13},{1... | collective-permute-start | bytes 147464 | tf_op jit(solution)/shard_map/ppermute | solution.py:14
  119.5 6.9 %collective-permute-start.5 = (f32[2,1,48,128]{3,2,1,0:T(8,128)S(1)}, f32[2,1,48,128]{3,2,1,0:T(8,128)S(1)}, u32[]{:S(2)}, u32[]{:S(2)}) collective-permute-start(f32[2,1,48,128]{3,2,1,0:T(8,128)S(1)} %get-tuple-element.34), channel_id=1, source_target_pairs={{4,0},{5,1},{6,2},{7,3},{8,4},{9,5},{10,6},{11,7},{12,8},{13,9},{1... | collective-permute-start | bytes 147464 | tf_op jit(solution)/shard_map/ppermute | solution.py:14
  120.8 22.2 %collective-permute-start.3 = (f32[2,3,24,12,128]{4,2,3,1,0:T(8,128)S(1)}, f32[2,3,24,12,128]{4,2,3,1,0:T(8,128)S(1)}, u32[]{:S(2)}, u32[]{:S(2)}) collective-permute-start(f32[2,3,24,12,128]{4,2,3,1,0:T(8,128)S(1)} %get-tuple-element.16), channel_id=1, source_target_pairs={{1,0},{2,1},{3,2},{4,3},{5,4},{6,5},{7,6},{8,7},{9,8},{10,9},{11,1... | collective-permute-start | bytes 2654216 | tf_op jit(solution)/shard_map/ppermute | solution.py:14
  122.1 5.0 %copy-start.6 = (f32[2,1,48,128]{3,2,1,0:T(8,128)}, f32[2,1,48,128]{3,2,1,0:T(8,128)S(1)}, u32[]{:S(2)}) copy-start(f32[2,1,48,128]{3,2,1,0:T(8,128)S(1)} %collective-permute-done.4) | copy-start | bytes 147460
  126.5 0.7 copy-start.8
  127.1 5.4 %collective-permute-start.6 = (f32[2,26,1,128]{3,2,1,0:T(1,128)}, f32[2,26,1,128]{3,2,1,0:T(1,128)}, u32[]{:S(2)}, u32[]{:S(2)}) collective-permute-start(f32[2,26,1,128]{3,2,1,0:T(1,128)} %get-tuple-element.25), channel_id=1, source_target_pairs={{0,1},{1,2},{2,3},{3,4},{4,5},{5,6},{6,7},{7,8},{8,9},{9,10},{10,1... | collective-permute-start | bytes 79880 | tf_op jit(solution)/shard_map/ppermute | solution.py:14
  131.1 11.8 %collective-permute-start.7 = (f32[2,26,1,128]{3,2,1,0:T(1,128)}, f32[2,26,1,128]{3,2,1,0:T(1,128)S(1)}, u32[]{:S(2)}, u32[]{:S(2)}) collective-permute-start(f32[2,26,1,128]{3,2,1,0:T(1,128)} %get-tuple-element.26), channel_id=1, source_target_pairs={{1,0},{2,1},{3,2},{4,3},{5,4},{6,5},{7,6},{8,7},{9,8},{10,9},{11,1... | collective-permute-start | bytes 79880 | tf_op jit(solution)/shard_map/ppermute | solution.py:14
  142.9 2.0 copy-start.1
  150.6 3.9 copy-start.3
  150.6 3.9 copy-start.4
  150.6 3.9 copy-start.7
  150.6 3.9 copy-start.9
  156.0 30.7 %copy-start.11 = (s32[2,1]{0,1:T(1,128)S(1)}, s32[2,1]{0,1:T(1,128)}, u32[]{:S(2)}) copy-start(s32[2,1]{0,1:T(1,128)} %param.6) | copy-start | bytes 28
  156.1 23.4 %collective-permute-start.8 = (f32[2,1,48,128]{3,2,1,0:T(8,128)S(1)}, f32[2,1,48,128]{3,2,1,0:T(8,128)S(1)}, u32[]{:S(2)}, u32[]{:S(2)}) collective-permute-start(f32[2,1,48,128]{3,2,1,0:T(8,128)S(1)} %get-tuple-element.31), channel_id=1, source_target_pairs={{0,4},{1,5},{2,6},{3,7},{4,8},{5,9},{6,10},{7,11},{8,12},{9,13},{1... | collective-permute-start | bytes 147464 | tf_op jit(solution)/shard_map/ppermute | solution.py:14
  178.1 7.2 %collective-permute-start.9 = (f32[2,1,48,128]{3,2,1,0:T(8,128)S(1)}, f32[2,1,48,128]{3,2,1,0:T(8,128)S(1)}, u32[]{:S(2)}, u32[]{:S(2)}) collective-permute-start(f32[2,1,48,128]{3,2,1,0:T(8,128)S(1)} %get-tuple-element.32), channel_id=1, source_target_pairs={{4,0},{5,1},{6,2},{7,3},{8,4},{9,5},{10,6},{11,7},{12,8},{13,9},{1... | collective-permute-start | bytes 147464 | tf_op jit(solution)/shard_map/ppermute | solution.py:14
  185.4 2.6 collective-permute-start.10
  186.7 4.6 %collective-permute-start.11 = (f32[2,26,1,128]{3,2,1,0:T(1,128)S(1)}, f32[2,26,1,128]{3,2,1,0:T(1,128)S(1)}, u32[]{:S(2)}, u32[]{:S(2)}) collective-permute-start(f32[2,26,1,128]{3,2,1,0:T(1,128)S(1)} %get-tuple-element.24), channel_id=1, source_target_pairs={{1,0},{2,1},{3,2},{4,3},{5,4},{6,5},{7,6},{8,7},{9,8},{10,9},{11,1... | collective-permute-start | bytes 79880 | tf_op jit(solution)/shard_map/ppermute | solution.py:14
  192.9 10.2 %collective-permute-start.12 = (f32[2,1,48,128]{3,2,1,0:T(8,128)S(1)}, f32[2,1,48,128]{3,2,1,0:T(8,128)S(1)}, u32[]{:S(2)}, u32[]{:S(2)}) collective-permute-start(f32[2,1,48,128]{3,2,1,0:T(8,128)S(1)} %get-tuple-element.29), channel_id=1, source_target_pairs={{0,4},{1,5},{2,6},{3,7},{4,8},{5,9},{6,10},{7,11},{8,12},{9,13},{1... | collective-permute-start | bytes 147464 | tf_op jit(solution)/shard_map/ppermute | solution.py:14
  201.7 6.5 %collective-permute-start.13 = (f32[2,1,48,128]{3,2,1,0:T(8,128)S(1)}, f32[2,1,48,128]{3,2,1,0:T(8,128)S(1)}, u32[]{:S(2)}, u32[]{:S(2)}) collective-permute-start(f32[2,1,48,128]{3,2,1,0:T(8,128)S(1)} %get-tuple-element.30), channel_id=1, source_target_pairs={{4,0},{5,1},{6,2},{7,3},{8,4},{9,5},{10,6},{11,7},{12,8},{13,9},{1... | collective-permute-start | bytes 147464 | tf_op jit(solution)/shard_map/ppermute | solution.py:14
  208.3 10.7 %collective-permute-start.14 = (f32[2,26,1,128]{3,2,1,0:T(1,128)S(1)}, f32[2,26,1,128]{3,2,1,0:T(1,128)S(1)}, u32[]{:S(2)}, u32[]{:S(2)}) collective-permute-start(f32[2,26,1,128]{3,2,1,0:T(1,128)S(1)} %get-tuple-element.21), channel_id=1, source_target_pairs={{0,1},{1,2},{2,3},{3,4},{4,5},{5,6},{6,7},{7,8},{8,9},{9,10},{10,1... | collective-permute-start | bytes 79880 | tf_op jit(solution)/shard_map/ppermute | solution.py:14
  210.4 22.2 %collective-permute-start.20 = (f32[2,3,1,48,128]{4,3,2,1,0:T(8,128)S(1)}, f32[2,3,1,48,128]{4,3,2,1,0:T(8,128)S(1)}, u32[]{:S(2)}, u32[]{:S(2)}) collective-permute-start(f32[2,3,1,48,128]{4,3,2,1,0:T(8,128)S(1)} %get-tuple-element.14), channel_id=1, source_target_pairs={{4,0},{5,1},{6,2},{7,3},{8,4},{9,5},{10,6},{11,7},{12,8},{13,9},{1... | collective-permute-start | bytes 442376 | tf_op jit(solution)/shard_map/ppermute | solution.py:14
  211.7 20.9 %collective-permute-start.21 = (f32[2,3,1,48,128]{4,3,2,1,0:T(8,128)S(1)}, f32[2,3,1,48,128]{4,3,2,1,0:T(8,128)S(1)}, u32[]{:S(2)}, u32[]{:S(2)}) collective-permute-start(f32[2,3,1,48,128]{4,3,2,1,0:T(8,128)S(1)} %get-tuple-element.13), channel_id=1, source_target_pairs={{0,4},{1,5},{2,6},{3,7},{4,8},{5,9},{6,10},{7,11},{8,12},{9,13},{1... | collective-permute-start | bytes 442376 | tf_op jit(solution)/shard_map/ppermute | solution.py:14
  217.6 4.9 %collective-permute-start.15 = (f32[2,26,1,128]{3,2,1,0:T(1,128)S(1)}, f32[2,26,1,128]{3,2,1,0:T(1,128)S(1)}, u32[]{:S(2)}, u32[]{:S(2)}) collective-permute-start(f32[2,26,1,128]{3,2,1,0:T(1,128)S(1)} %get-tuple-element.22), channel_id=1, source_target_pairs={{1,0},{2,1},{3,2},{4,3},{5,4},{6,5},{7,6},{8,7},{9,8},{10,9},{11,1... | collective-permute-start | bytes 79880 | tf_op jit(solution)/shard_map/ppermute | solution.py:14
  224.1 14.0 %collective-permute-start.16 = (f32[2,1,48,128]{3,2,1,0:T(8,128)S(1)}, f32[2,1,48,128]{3,2,1,0:T(8,128)S(1)}, u32[]{:S(2)}, u32[]{:S(2)}) collective-permute-start(f32[2,1,48,128]{3,2,1,0:T(8,128)S(1)} %get-tuple-element.27), channel_id=1, source_target_pairs={{0,4},{1,5},{2,6},{3,7},{4,8},{5,9},{6,10},{7,11},{8,12},{9,13},{1... | collective-permute-start | bytes 147464 | tf_op jit(solution)/shard_map/ppermute | solution.py:14
  231.3 6.8 %collective-permute-start.17 = (f32[2,1,48,128]{3,2,1,0:T(8,128)S(1)}, f32[2,1,48,128]{3,2,1,0:T(8,128)S(1)}, u32[]{:S(2)}, u32[]{:S(2)}) collective-permute-start(f32[2,1,48,128]{3,2,1,0:T(8,128)S(1)} %get-tuple-element.28), channel_id=1, source_target_pairs={{4,0},{5,1},{6,2},{7,3},{8,4},{9,5},{10,6},{11,7},{12,8},{13,9},{1... | collective-permute-start | bytes 147464 | tf_op jit(solution)/shard_map/ppermute | solution.py:14
  232.8 8.9 %collective-permute-start.22 = (f32[2,3,26,1,128]{4,3,2,1,0:T(1,128)S(1)}, f32[2,3,26,1,128]{4,3,2,1,0:T(1,128)S(1)}, u32[]{:S(2)}, u32[]{:S(2)}) collective-permute-start(f32[2,3,26,1,128]{4,3,2,1,0:T(1,128)S(1)} %get-tuple-element.11), channel_id=1, source_target_pairs={{1,0},{2,1},{3,2},{4,3},{5,4},{6,5},{7,6},{8,7},{9,8},{10,9},{11,1... | collective-permute-start | bytes 239624 | tf_op jit(solution)/shard_map/ppermute | solution.py:14
  234.1 7.7 %collective-permute-start.23 = (f32[2,3,26,1,128]{4,3,2,1,0:T(1,128)S(1)}, f32[2,3,26,1,128]{4,3,2,1,0:T(1,128)S(1)}, u32[]{:S(2)}, u32[]{:S(2)}) collective-permute-start(f32[2,3,26,1,128]{4,3,2,1,0:T(1,128)S(1)} %get-tuple-element.12), channel_id=1, source_target_pairs={{0,1},{1,2},{2,3},{3,4},{4,5},{5,6},{6,7},{7,8},{8,9},{9,10},{10,1... | collective-permute-start | bytes 239624 | tf_op jit(solution)/shard_map/ppermute | solution.py:14
  238.1 3.7 collective-permute-start.18
  240.4 8.7 %collective-permute-start.19 = (f32[2,26,1,128]{3,2,1,0:T(1,128)S(1)}, f32[2,26,1,128]{3,2,1,0:T(1,128)S(1)}, u32[]{:S(2)}, u32[]{:S(2)}) collective-permute-start(f32[2,26,1,128]{3,2,1,0:T(1,128)S(1)} %get-tuple-element.20), channel_id=1, source_target_pairs={{1,0},{2,1},{3,2},{4,3},{5,4},{6,5},{7,6},{8,7},{9,8},{10,9},{11,1... | collective-permute-start | bytes 79880 | tf_op jit(solution)/shard_map/ppermute | solution.py:14
  398.6 1.0 copy-start.5
Sparse Core Ops, SparseCore 0:
  254.4 142.8 all-reduce.7
where the time goes:
time: 408 us; the launch traced here: 406 us
  waiting for transfers between devices  258 us (63%)
  starting transfers between devices  87.7 us (21%)
  other arithmetic  16.9 us (4%)
  between operations  16.7 us (4%)
  matrix products  14.6 us (4%)
  local copies, waits for them, and re-layouts  12.5 us (3%)
    psum x1, waiting for transfers between devices, per_device(): numer_all, denom_all = lax.psum((numer, denom), 'subj')  143 us
    ppermute x24, waiting for transfers between devices, shifted(): return lax.ppermute(shard, axis, pairs)  115 us
    ppermute x24, starting transfers between devices, shifted(): return lax.ppermute(shard, axis, pairs)  87.6 us
  transfers between devices with their start and end apart: 25, of which 10 were waited for; matrix products, arithmetic and copies ran while one was open for 2% of the time, Pallas kernels for 0%

commit v1 on v0

v1 whole, which is shorter than its diff:
```python
import functools

import jax
import jax.numpy as jnp
from jax import lax
from jax.experimental import pallas as pl
from jax.experimental.pallas import tpu as pltpu
from jax.sharding import PartitionSpec as P

TGY = 4
STEPS = 4
CX = 24
CY = 48
CZ = 128
EDGE = 16
PAD = 8
MESH = pl.DeviceIdType.MESH
OWN = slice(PAD, PAD + CY)
N, S, W, E = range(4)


def kernel(
    wide,
    widths_ref,
    flags_ref,
    image_ref,
    moment_ref,
    mismatch_ref,
    template_ref,
    edge_out,
    edge_in,
    field,
    speed,
    warped,
    rows_in,
    cols_out,
    cols_in,
    vrows_in,
    vcols_out,
    vcols_in,
    weight,
    sums,
    pair_in,
    half,
    parts_in,
    whole,
    z_send,
    z_recv,
    y_send,
    y_recv,
    step_send,
    step_recv,
    v_send,
    v_recv,
    pair_send,
    pair_recv,
    part_send,
    part_recv,
    gather_send,
    gather_recv,
):
    subj = lax.axis_index("subj")
    space = lax.axis_index("space")
    row, col = space // TGY, space % TGY
    chip, core = subj // 2, subj % 2
    place = (
        (subj, ((row + 3) % 4) * TGY + col),
        (subj, ((row + 1) % 4) * TGY + col),
        (subj, row * TGY + (col + 3) % 4),
        (subj, row * TGY + (col + 1) % 4),
    )
    sibling = (chip * 2 + 1 - core, space)
    chips = [(chip + k) % 8 for k in range(1, 8)]
    peers = [(other * 2 + core, space) for other in chips]

    barrier = pltpu.get_barrier_semaphore()
    for device in list(place) + [sibling] + peers:
        pl.semaphore_signal(barrier, inc=1, device_id=device, device_id_type=MESH)

    has = tuple(
        jnp.where(flag, 1.0, 0.0).astype(jnp.float32)
        for flag in (row > 0, row < 3, col > 0, col < TGY - 1)
    )
    lane = lax.broadcasted_iota(jnp.int32, (8, CZ), 1)
    tiles = [(PAD + 8 * t, 8 * t) for t in range(CY // 8)]

    def remote(src, dst, send, recv, device):
        return pltpu.make_async_remote_copy(
            src_ref=src,
            dst_ref=dst,
            send_sem=send,
            recv_sem=recv,
            device_id=device,
            device_id_type=MESH,
        )

    def loop(body, count, unroll=1):
        def step(i, carry):
            body(i)
            return carry

        lax.fori_loop(0, count, step, 0, unroll=unroll)

    def stage_edges(c):
        def body(x):
            edge_out[c, 0, x] = moment_ref[c, x, 0:EDGE, :].astype(jnp.float32)
            edge_out[c, 1, x] = moment_ref[c, x, CY - EDGE : CY, :].astype(jnp.float32)

        loop(body, CX, 4)

    def stage_image(s):
        def body(x):
            value = image_ref[s, x].astype(jnp.float32)
            warped[s, 0, x + 1, OWN, :] = value
            cols_out[s, 0, 0, pl.ds(x, 1), :] = value[0:1]
            cols_out[s, 0, 1, pl.ds(x, 1), :] = value[CY - 1 : CY]

        loop(body, CX, 4)

    for c in range(6):
        stage_edges(c)
    for s in range(2):
        stage_image(s)
    pl.semaphore_wait(barrier, 12)

    def start_edges(c):
        pair = (
            remote(edge_out.at[c, 0], edge_in.at[c, 1], y_send.at[c, 0], y_recv.at[c, 0], place[W]),
            remote(edge_out.at[c, 1], edge_in.at[c, 0], y_send.at[c, 1], y_recv.at[c, 1], place[E]),
        )
        for copy in pair:
            copy.start()
        return pair

    def start_halo(s, k):
        slot = k % 2
        copies = (
            remote(warped.at[s, slot, 1, OWN], rows_in.at[s, k, 1], step_send.at[s, k, N], step_recv.at[s, k, N], place[N]),
            remote(warped.at[s, slot, CX, OWN], rows_in.at[s, k, 0], step_send.at[s, k, S], step_recv.at[s, k, S], place[S]),
            remote(cols_out.at[s, k, 0], cols_in.at[s, k, 1], step_send.at[s, k, W], step_recv.at[s, k, W], place[W]),
            remote(cols_out.at[s, k, 1], cols_in.at[s, k, 0], step_send.at[s, k, E], step_recv.at[s, k, E], place[E]),
        )
        for copy in copies:
            copy.start()
        return copies

    def start_speed(s):
        a, b = 3 * s, 3 * s + 1
        del b
        copies = (
            remote(speed.at[a, 1, OWN], vrows_in.at[s, 1], v_send.at[s, N], v_recv.at[s, N], place[N]),
            remote(speed.at[a, CX, OWN], vrows_in.at[s, 0], v_send.at[s, S], v_recv.at[s, S], place[S]),
            remote(vcols_out.at[s, 0], vcols_in.at[s, 1], v_send.at[s, W], v_recv.at[s, W], place[W]),
            remote(vcols_out.at[s, 1], vcols_in.at[s, 0], v_send.at[s, E], v_recv.at[s, E], place[E]),
        )
        for copy in copies:
            copy.start()
        return copies

    def start_bulk(c):
        copies = (
            remote(field.at[c, pl.ds(wide, wide)], field.at[c, pl.ds(wide + CX, wide)], z_send.at[c, 0], z_recv.at[c, 0], place[N]),
            remote(field.at[c, pl.ds(CX, wide)], field.at[c, pl.ds(0, wide)], z_send.at[c, 1], z_recv.at[c, 1], place[S]),
        )
        for copy in copies:
            copy.start()
        return copies

    edges = [start_edges(0)]
    halos = {(s, 0): start_halo(s, 0) for s in range(2)}
    edges += [start_edges(c) for c in range(1, 6)]

    width = [widths_ref[a].astype(jnp.float32) for a in range(3)]
    out_id = lax.broadcasted_iota(jnp.int32, (CY, CY + 2 * EDGE), 0)
    in_id = lax.broadcasted_iota(jnp.int32, (CY, CY + 2 * EDGE), 1)
    dist = jnp.abs(in_id - EDGE - out_id).astype(jnp.float32)
    second = jnp.maximum(width[1] + 1.0 - dist, 0.0)
    second = jnp.where(in_id < EDGE, second * has[W], second)
    second = jnp.where(in_id >= EDGE + CY, second * has[E], second)
    second = second.astype(jnp.bfloat16)
    out_id = lax.broadcasted_iota(jnp.int32, (CZ, CZ), 0)
    in_id = lax.broadcasted_iota(jnp.int32, (CZ, CZ), 1)
    dist = jnp.abs(in_id - out_id).astype(jnp.float32)
    third = jnp.maximum(width[2] + 1.0 - dist, 0.0).astype(jnp.bfloat16)
    norm = 1.0
    for a in range(3):
        norm = norm * ((width[a] + 1.0) * (width[a] + 1.0))
    scale = jnp.full((8, CZ), 1.0 / STEPS, jnp.float32) / jnp.full((8, CZ), 1.0, jnp.float32) / norm

    def smooth_inner(c):
        group = 4

        def body(g):
            blocks = []
            for j in range(group):
                x = g * group + j
                ext = jnp.concatenate(
                    [
                        edge_in[c, 0, x].astype(jnp.bfloat16),
                        moment_ref[c, x],
                        edge_in[c, 1, x].astype(jnp.bfloat16),
                    ],
                    axis=0,
                )
                blocks.append(jnp.dot(second, ext, preferred_element_type=jnp.float32))
            value = jnp.concatenate(blocks, axis=0)
            high = value.astype(jnp.bfloat16)
            low = (value - high.astype(jnp.float32)).astype(jnp.bfloat16)
            value = jnp.dot(high, third, preferred_element_type=jnp.float32) + jnp.dot(
                low, third, preferred_element_type=jnp.float32
            )
            for j in range(group):
                field[c, wide + g * group + j] = value[j * CY : (j + 1) * CY]

        loop(body, CX // group)

    def smooth_first(c):
        s, a = c // 3, c % 3

        def at(i, t, side=None):
            value = field[c, i, t : t + 8, :]
            return value if side is None else value * has[side]

        total, slope = [], []
        for _, t in tiles:
            sides = [N] * wide + [None] * CX
            first = [at(i, t, sides[i]) for i in range(2 * wide + 2)]
            total.append(sum((wide + 1.0 - abs(i - wide)) * first[i] for i in range(2 * wide + 1)))
            slope.append(sum(first[wide + 1 : 2 * wide + 2]) - sum(first[0 : wide + 1]))

        def emit(x, values):
            for (p, _), value in zip(tiles, values):
                speed[c, x + 1, p : p + 8, :] = value * scale
            if a == 1:
                vcols_out[s, 0, pl.ds(x, 1), :] = (values[0] * scale)[0:1]
                vcols_out[s, 1, pl.ds(x, 1), :] = (values[-1] * scale)[7:8]

        def advance(low, high):
            def step(i, carry):
                total, slope = carry
                emit(i, total)
                total = [p + q for p, q in zip(total, slope)]
                ahead = jnp.where(i + 2 * wide + 2 >= wide + CX, has[S], 1.0)
                behind = jnp.where(i < wide, has[N], 1.0)
                slope = [
                    q + (at(i + 2 * wide + 2, t) * ahead + at(i, t) * behind - 2.0 * at(i + wide + 1, t))
                    for q, (_, t) in zip(slope, tiles)
                ]
                return total, slope

            return lambda carry: lax.fori_loop(low, high, step, carry)

        total, slope = advance(0, CX - 2)((total, slope))
        emit(CX - 2, total)
        emit(CX - 1, [p + q for p, q in zip(total, slope)])

    def side_columns(target, columns, x):
        target[x + 1, PAD - 1 : PAD, :] = columns[0, pl.ds(x, 1), :] * has[W]
        target[x + 1, PAD + CY : PAD + CY + 1, :] = columns[1, pl.ds(x, 1), :] * has[E]

    def side_rows(target, rows):
        target[0, OWN, :] = rows[0] * has[N]
        target[CX + 1, OWN, :] = rows[1] * has[S]

    def transport(s, k, after):
        held, made = warped.at[s, k % 2], warped.at[s, (k + 1) % 2]
        side_rows(held, rows_in.at[s, k])

        def body(x):
            side_columns(held, cols_in.at[s, k], x)
            values = []
            for p, _ in tiles:
                centre = held[x + 1, p : p + 8, :]
                below = jnp.where(lane == 0, 0.0, pltpu.roll(centre, 1, 1))
                above = jnp.where(lane == CZ - 1, 0.0, pltpu.roll(centre, CZ - 1, 1))
                sides = (
                    (held[x, p : p + 8, :], held[x + 2, p : p + 8, :]),
                    (held[x + 1, p - 1 : p + 7, :], held[x + 1, p + 1 : p + 9, :]),
                    (below, above),
                )
                value = centre
                for a in range(3):
                    rate = speed[3 * s + a, x + 1, p : p + 8, :]
                    lower, upper = sides[a]
                    value = value - jnp.abs(rate) * (centre - jnp.where(rate > 0.0, lower, upper))
                made[x + 1, p : p + 8, :] = value
                values.append(value)
            after(x, values)

        loop(body, CX, 2)

    def stage_columns(s, k):
        def after(x, values):
            cols_out[s, k, 0, pl.ds(x, 1), :] = values[0][0:1]
            cols_out[s, k, 1, pl.ds(x, 1), :] = values[-1][7:8]

        return after

    def wait(copies):
        for copy in copies:
            copy.wait()

    def weigh(s):
        first, middle, last = (speed.at[3 * s + a] for a in range(3))
        side_rows(first, vrows_in.at[s])
        flag = flags_ref[s].astype(jnp.float32)

        def body(x):
            side_columns(middle, vcols_in.at[s], x)
            for p, t in tiles:
                centre = last[x + 1, p : p + 8, :]
                below = jnp.where(lane == 0, 0.0, pltpu.roll(centre, 1, 1))
                above = jnp.where(lane == CZ - 1, 0.0, pltpu.roll(centre, CZ - 1, 1))
                total = first[x + 2, p : p + 8, :] - first[x, p : p + 8, :]
                total = total + (middle[x + 1, p + 1 : p + 9, :] - middle[x + 1, p - 1 : p + 7, :])
                total = total + (above - below)
                value = flag * jnp.exp(total * (0.5 * STEPS))
                weight[s, x, t : t + 8, :] = value
                if s == 0:
                    sums[1, x, t : t + 8, :] = value
                else:
                    sums[1, x, t : t + 8, :] += value

        loop(body, CX, 2)

    mine = pl.multiple_of(24 * core, 8)
    theirs = pl.multiple_of(24 * (1 - core), 8)

    def start_pair(q):
        copy = remote(sums.at[q, :, pl.ds(theirs, 24)], pair_in.at[q], pair_send.at[q], pair_recv.at[q], sibling)
        copy.start()
        return copy

    def start_parts(q):
        def body(x):
            half[q, x] = sums[q, x, pl.ds(mine, 24), :] + pair_in[q, x]

        loop(body, CX, 4)
        copies = [
            remote(half.at[q, pl.ds(3 * other, 3)], parts_in.at[q, k], part_send.at[q, k], part_recv.at[q, k], peers[k])
            for k, other in enumerate(chips)
        ]
        for copy in copies:
            copy.start()
        return copies

    bulk = {}
    for c in range(6):
        wait(edges[c])
        smooth_inner(c)
        if c < 4:
            bulk[c] = start_bulk(c)
    for c in range(3):
        wait(bulk[c])
        smooth_first(c)
    for k in range(4):
        wait(halos[0, k])
        if k == 1:
            wait(shift)
        if k < 3:
            transport(0, k, stage_columns(0, k + 1))
            halos[0, k + 1] = start_halo(0, k + 1)
            if k == 0:
                shift = start_speed(0)
            if k < 2:
                bulk[4 + k] = start_bulk(4 + k)
        else:
            transport(0, k, lambda x, values: None)
        if k == 1:
            weigh(0)
            wait(bulk[3])
            smooth_first(3)
        if k == 2:
            wait(bulk[4])
            smooth_first(4)

    wait(bulk[5])
    smooth_first(5)
    wait(halos[1, 0])
    transport(1, 0, stage_columns(1, 1))
    halos[1, 1] = start_halo(1, 1)
    shift = start_speed(1)
    wait(halos[1, 1])
    transport(1, 1, stage_columns(1, 2))
    halos[1, 2] = start_halo(1, 2)
    wait(shift)
    weigh(1)
    pair = start_pair(1)
    wait(halos[1, 2])
    transport(1, 2, stage_columns(1, 3))
    halos[1, 3] = start_halo(1, 3)
    pair.wait()
    parts = start_parts(1)
    wait(halos[1, 3])

    def gather_sum(x, values):
        for (p, t), value in zip(tiles, values):
            sums[0, x, t : t + 8, :] = (
                weight[0, x, t : t + 8, :] * warped[0, 0, x + 1, p : p + 8, :] + weight[1, x, t : t + 8, :] * value
            )

    transport(1, 3, gather_sum)
    pair = start_pair(0)
    wait(parts)
    pair.wait()
    wait(start_parts(0))

    own = 3 * chip
    for x in range(3):
        total = [half[q, own + x] for q in range(2)]
        for q in range(2):
            for k in range(7):
                total[q] = total[q] + parts_in[q, k, x]
        whole[own + x, pl.ds(mine, 24), :] = total[0] / (1.0 + total[1])

    def piece(other):
        return whole.at[pl.ds(3 * other, 3), pl.ds(mine, 24)]

    copies = [remote(piece(chip), piece(chip), gather_send.at[k], gather_recv.at[k], peers[k]) for k in range(7)]
    onward = [remote(piece(chip), piece(chip), gather_send.at[7], gather_recv.at[7], sibling)]
    for copy in copies + onward:
        copy.start()
    for k in range(7):
        copies[k].wait_recv()
        block = piece((chip + 7 - k) % 8)
        onward.append(remote(block, block, gather_send.at[8 + k], gather_recv.at[8 + k], sibling))
        onward[-1].start()
    for copy in copies:
        copy.wait_send()
    wait(onward)

    def finish(x):
        value = whole[x]
        template_ref[x] = value
        for s in range(2):
            mismatch_ref[s, x] = (warped[s, 0, x + 1, OWN, :] - value).astype(jnp.bfloat16)

    loop(finish, CX, 4)


def build(index, wide):
    f32 = jnp.float32
    dma = pltpu.SemaphoreType.DMA
    return pl.pallas_call(
        functools.partial(kernel, wide),
        out_shape=(
            jax.ShapeDtypeStruct((2, CX, CY, CZ), jnp.bfloat16),
            jax.ShapeDtypeStruct((CX, CY, CZ), f32),
        ),
        in_specs=[pl.BlockSpec(memory_space=pltpu.SMEM)] * 2 + [pl.BlockSpec(memory_space=pltpu.VMEM)] * 2,
        out_specs=(pl.BlockSpec(memory_space=pltpu.VMEM),) * 2,
        scratch_shapes=[
            pltpu.VMEM((6, 2, CX, EDGE, CZ), f32),
            pltpu.VMEM((6, 2, CX, EDGE, CZ), f32),
            pltpu.VMEM((6, CX + 2 * wide, CY, CZ), f32),
            pltpu.VMEM((6, CX + 2, CY + 2 * PAD, CZ), f32),
            pltpu.VMEM((2, 2, CX + 2, CY + 2 * PAD, CZ), f32),
            pltpu.VMEM((2, 4, 2, CY, CZ), f32),
            pltpu.VMEM((2, 4, 2, CX, CZ), f32),
            pltpu.VMEM((2, 4, 2, CX, CZ), f32),
            pltpu.VMEM((2, 2, CY, CZ), f32),
            pltpu.VMEM((2, 2, CX, CZ), f32),
            pltpu.VMEM((2, 2, CX, CZ), f32),
            pltpu.VMEM((2, CX, CY, CZ), f32),
            pltpu.VMEM((2, CX, CY, CZ), f32),
            pltpu.VMEM((2, CX, 24, CZ), f32),
            pltpu.VMEM((2, CX, 24, CZ), f32),
            pltpu.VMEM((2, 7, 3, 24, CZ), f32),
            pltpu.VMEM((CX, CY, CZ), f32),
            dma((6, 2)),
            dma((6, 2)),
            dma((6, 2)),
            dma((6, 2)),
            dma((2, 4, 4)),
            dma((2, 4, 4)),
            dma((2, 4)),
            dma((2, 4)),
            dma((2,)),
            dma((2,)),
            dma((2, 7)),
            dma((2, 7)),
            dma((15,)),
            dma((15,)),
        ],
        compiler_params=pltpu.CompilerParams(
            collective_id=index, has_side_effects=True, vmem_limit_bytes=48 * 2**20
        ),
    )


def per_device(image, momentum, tissue_flags, band_widths):
    args = (
        band_widths,
        tissue_flags.reshape(2),
        image.reshape(2, CX, CY, CZ),
        momentum.reshape(6, CX, CY, CZ),
    )
    which = jnp.clip((band_widths[0] - 8) // 2, 0, 2)
    mismatch, template = lax.switch(which, [build(i, 8 + 2 * i) for i in range(3)], *args)
    return mismatch[:, None], template[None]


def solution(mesh):
    return jax.shard_map(
        per_device,
        mesh=mesh,
        in_specs=(
            P("subj", "space", None, None, None),
            P("subj", None, "space", None, None, None),
            P("subj", "space"),
            P(),
        ),
        out_specs=(P("subj", "space", None, None, None), P("space", None, None, None)),
        check_vma=False,
    )
```

time: 408 us -> 129 us (0.32)
  waiting for transfers between devices: 258 us -> 0 us
  Pallas kernels: 0 us -> 126 us
  starting transfers between devices: 87.7 us -> 0 us
  other arithmetic: 16.9 us -> 0 us
  between operations: 16.7 us -> 1.31 us
  matrix products: 14.6 us -> 0 us
  local copies, waits for them, and re-layouts: 12.5 us -> 1.63 us
    psum x1 -> x0, waiting for transfers between devices: 143 us -> none  [per_device(): numer_all, denom_all = lax.psum((numer, denom), 'subj')]
    pallas_call x0 -> x1, Pallas kernels: none -> 126 us  [per_device(): lax.switch(which, [build(i, 8 + 2 * i) for i in range(3)], *args)]
    ppermute x24 -> x0, waiting for transfers between devices: 115 us -> none  [shifted(): return lax.ppermute(shard, axis, pairs)]
    ppermute x24 -> x0, starting transfers between devices: 87.6 us -> none  [shifted(): return lax.ppermute(shard, axis, pairs)]
    dot_general x3 -> x0, matrix products: 14.6 us -> none  [the longest x1 5.48 us: smooth_first(): jnp.einsum('ij,abjyz->abiyz', matrix, field, precision=lax.Precision.HIGH...]
    reduce_sum x1 -> x0, other arithmetic: 5.23 us -> none  [per_device(): denom = jnp.sum(weight, axis=0)]
    slice x10 -> x0, local copies, waits for them, and re-layouts: 4.86 us -> none  [the longest x7 2.3 us: extend(): north = shifted(field[..., -wide_x:, :, :], 'space', TGY)]
    sub x5 -> x0, other arithmetic: 4.61 us -> none  [the longest x3 4.61 us: advance(): return centre - 1.0 / STEPS * flux]
  transfers between devices with their start and end apart: 25 -> 0, of which waited for: 10 -> 0; matrix products, arithmetic and copies ran while one was open for 2% -> 0% of each run, Pallas kernels for 0% -> 0%
where the time goes in v1:
time: 129 us
  Pallas kernels  126 us (98%)
  local copies, waits for them, and re-layouts  1.63 us (1%)
  between operations  1.31 us (1%)
    pallas_call x1, Pallas kernels, per_device(): lax.switch(which, [build(i, 8 + 2 * i) for i in range(3)], *args)  126 us

profile of v1, /device:TPU:1, one launch (start us, length us, event | category | flops | bytes accessed | tf_op | source)
XLA Modules:
  0.0 128.8 jit_solution(11236145961356252699)
XLA Ops:
  1.3 125.8 %conditional.1 = ((bf16[2,24,48,128]{3,2,1,0:T(8,128)(2,1)S(1)}, f32[24,48,128]{2,1,0:T(8,128)S(1)})) conditional(s32[]{:T(128)} %clamp.3, (s32[3]{0:T(128)}, s32[2]{0:T(128)}, bf16[2,24,48,128]{3,2,1,0:T(8,128)(2,1)}, bf16[6,24,48,128]{3,2,1,0:T(8,128)(2,1)}) %tuple.44, (s32[3]{0:T(128)}, s32[2]{0:T(128)}, ...), branch_computations={%region_0.1_spmd, %region_1.2_spmd, %region_2.3_spmd} | conditional | bytes 8 | solution.py:499
  1.3 125.8 %branch_1_fun.1 = (bf16[2,24,48,128]{3,2,1,0:T(8,128)(2,1)S(1)}, f32[24,48,128]{2,1,0:T(8,128)S(1)}) custom-call(s32[3]{0:T(128)} %get-tuple-element.38.widths_ref, s32[2]{0:T(128)} %get-tuple-element.39.flags_ref, bf16[2,24,48,128]{3,2,1,0:T(8,128)(2,1)} %get-tuple-element.40.image_ref, bf16[6,24,48,128]{3,2,1,0:T(8,128)(2,1)} %get-tuple-element.41.moment_ref), custom_call_target="tpu_custom_call" | custom-call | tf_op jit(solution)/shard_map/cond/branch_1_fun/pallas_call | solution.py:499
  127.1 0.8 copy.14
  128.0 0.8 copy.15

commit v2 on v1

--- a/solution.py
+++ b/solution.py
@@ -23,13 +23,16 @@
     wide,
     widths_ref,
     flags_ref,
+    image_hbm,
+    moment_hbm,
+    mismatch_ref,
+    template_ref,
     image_ref,
     moment_ref,
-    mismatch_ref,
-    template_ref,
     edge_out,
     edge_in,
     field,
+    middle_field,
     speed,
     warped,
     rows_in,
@@ -43,7 +46,9 @@
     pair_in,
     half,
     parts_in,
+    denom_in,
     whole,
+    load,
     z_send,
     z_recv,
     y_send,
@@ -56,6 +61,8 @@
     pair_recv,
     part_send,
     part_recv,
+    denom_send,
+    denom_recv,
     gather_send,
     gather_recv,
 ):
@@ -69,13 +76,17 @@
         (subj, row * TGY + (col + 3) % 4),
         (subj, row * TGY + (col + 1) % 4),
     )
-    sibling = (chip * 2 + 1 - core, space)
-    chips = [(chip + k) % 8 for k in range(1, 8)]
-    peers = [(other * 2 + core, space) for other in chips]
+    owners = [((chip + b // 2 + 1) % 8, core if b % 2 == 0 else 1 - core) for b in range(14)]
+    owners.append((chip, 1 - core))
+    peers = [(chip_at * 2 + core_at, space) for chip_at, core_at in owners]
 
     barrier = pltpu.get_barrier_semaphore()
-    for device in list(place) + [sibling] + peers:
+    for device in list(place) + peers:
         pl.semaphore_signal(barrier, inc=1, device_id=device, device_id_type=MESH)
+    loads = [pltpu.make_async_copy(moment_hbm.at[c], moment_ref.at[c], load.at[c]) for c in range(6)]
+    loads.append(pltpu.make_async_copy(image_hbm, image_ref, load.at[6]))
+    for copy in loads:
+        copy.start()
 
     has = tuple(
         jnp.where(flag, 1.0, 0.0).astype(jnp.float32)
@@ -106,7 +117,7 @@
             edge_out[c, 0, x] = moment_ref[c, x, 0:EDGE, :].astype(jnp.float32)
             edge_out[c, 1, x] = moment_ref[c, x, CY - EDGE : CY, :].astype(jnp.float32)
 
-        loop(body, CX, 4)
+        loop(body, CX, 8)
 
     def stage_image(s):
         def body(x):
@@ -117,11 +128,15 @@
 
         loop(body, CX, 4)
 
-    for c in range(6):
+    def stage_first(x):
+        field[0, wide + x] = moment_ref[0, x].astype(jnp.float32)
+
+    loads[0].wait()
+    loop(stage_first, CX, 8)
+    for c in range(1, 4):
+        loads[c].wait()
         stage_edges(c)
-    for s in range(2):
-        stage_image(s)
-    pl.semaphore_wait(barrier, 12)
+    pl.semaphore_wait(barrier, 19)
 
     def start_edges(c):
         pair = (
@@ -144,12 +159,18 @@
             copy.start()
         return copies
 
-    def start_speed(s):
-        a, b = 3 * s, 3 * s + 1
-        del b
+    def start_speed_rows(s):
+        a = 3 * s
         copies = (
             remote(speed.at[a, 1, OWN], vrows_in.at[s, 1], v_send.at[s, N], v_recv.at[s, N], place[N]),
             remote(speed.at[a, CX, OWN], vrows_in.at[s, 0], v_send.at[s, S], v_recv.at[s, S], place[S]),
+        )
+        for copy in copies:
+            copy.start()
+        return copies
+
+    def start_speed_cols(s):
+        copies = (
             remote(vcols_out.at[s, 0], vcols_in.at[s, 1], v_send.at[s, W], v_recv.at[s, W], place[W]),
             remote(vcols_out.at[s, 1], vcols_in.at[s, 0], v_send.at[s, E], v_recv.at[s, E], place[E]),
         )
@@ -166,9 +187,25 @@
             copy.start()
         return copies
 
-    edges = [start_edges(0)]
-    halos = {(s, 0): start_halo(s, 0) for s in range(2)}
-    edges += [start_edges(c) for c in range(1, 6)]
+    def start_middle():
+        copies = (
+            remote(middle_field.at[:, 0:EDGE], edge_in.at[0, 1], y_send.at[0, 0], y_recv.at[0, 0], place[W]),
+            remote(middle_field.at[:, CY - EDGE : CY], edge_in.at[0, 0], y_send.at[0, 1], y_recv.at[0, 1], place[E]),
+        )
+        for copy in copies:
+            copy.start()
+        return copies
+
+    edges = {1: start_edges(1)}
+    bulk = {0: start_bulk(0)}
+    for c in range(2, 4):
+        edges[c] = start_edges(c)
+    for c in range(4, 6):
+        loads[c].wait()
+        stage_edges(c)
+    loads[6].wait()
+    for s in range(2):
+        stage_image(s)
 
     width = [widths_ref[a].astype(jnp.float32) for a in range(3)]
     out_id = lax.broadcasted_iota(jnp.int32, (CY, CY + 2 * EDGE), 0)
@@ -188,7 +225,7 @@
     scale = jnp.full((8, CZ), 1.0 / STEPS, jnp.float32) / jnp.full((8, CZ), 1.0, jnp.float32) / norm
 
     def smooth_inner(c):
-        group = 4
+        group = 12
 
         def body(g):
             blocks = []
@@ -214,6 +251,28 @@
 
         loop(body, CX // group)
 
+    def split(value):
+        high = value.astype(jnp.bfloat16)
+        return high, (value - high.astype(jnp.float32)).astype(jnp.bfloat16)
+
+    def smooth_inner_last():
+        group = 12
+
+        def body(g):
+            blocks = []
+            for j in range(group):
+                x = g * group + j
+                ext = jnp.concatenate([edge_in[0, 0, x], middle_field[x], edge_in[0, 1, x]], axis=0)
+                blocks.append(
+                    sum(jnp.dot(second, part, preferred_element_type=jnp.float32) for part in split(ext))
+                )
+            value = jnp.concatenate(blocks, axis=0)
+            value = sum(jnp.dot(part, third, preferred_element_type=jnp.float32) for part in split(value))
+            for j in range(group):
+                speed[0, g * group + j + 1, OWN, :] = value[j * CY : (j + 1) * CY] * scale[0:1]
+
+        loop(body, CX // group)
+
     def smooth_first(c):
         s, a = c // 3, c % 3
 
@@ -229,8 +288,11 @@
             slope.append(sum(first[wide + 1 : 2 * wide + 2]) - sum(first[0 : wide + 1]))
 
         def emit(x, values):
-            for (p, _), value in zip(tiles, values):
-                speed[c, x + 1, p : p + 8, :] = value * scale
+            for (p, t), value in zip(tiles, values):
+                if c == 0:
+                    middle_field[x, t : t + 8, :] = value
+                else:
+                    speed[c, x + 1, p : p + 8, :] = value * scale
             if a == 1:
                 vcols_out[s, 0, pl.ds(x, 1), :] = (values[0] * scale)[0:1]
                 vcols_out[s, 1, pl.ds(x, 1), :] = (values[-1] * scale)[7:8]
@@ -248,7 +310,7 @@
                 ]
                 return total, slope
 
-            return lambda carry: lax.fori_loop(low, high, step, carry)
+            return lambda carry: lax.fori_loop(low, high, step, carry, unroll=2)
 
         total, slope = advance(0, CX - 2)((total, slope))
         emit(CX - 2, total)
@@ -262,7 +324,7 @@
         target[0, OWN, :] = rows[0] * has[N]
         target[CX + 1, OWN, :] = rows[1] * has[S]
 
-    def transport(s, k, after):
+    def transport(s, k, after, blocks=None):
         held, made = warped.at[s, k % 2], warped.at[s, (k + 1) % 2]
         side_rows(held, rows_in.at[s, k])
 
@@ -287,7 +349,12 @@
                 values.append(value)
             after(x, values)
 
-        loop(body, CX, 2)
+        if blocks is None:
+            loop(body, CX, 8)
+        else:
+            for b, block in enumerate(blocks):
+                loop(lambda r: body(3 * block + r), 3, 3)
+                send_numer(b)
 
     def stage_columns(s, k):
         def after(x, values):
@@ -321,76 +388,110 @@
                 else:
                     sums[1, x, t : t + 8, :] += value
 
-        loop(body, CX, 2)
-
-    mine = pl.multiple_of(24 * core, 8)
-    theirs = pl.multiple_of(24 * (1 - core), 8)
-
-    def start_pair(q):
-        copy = remote(sums.at[q, :, pl.ds(theirs, 24)], pair_in.at[q], pair_send.at[q], pair_recv.at[q], sibling)
+        loop(body, CX, 8)
+
+    def piece(ref, chip_at, core_at):
+        return ref.at[pl.ds(3 * chip_at, 3), pl.ds(pl.multiple_of(24 * core_at, 8), 24)]
+
+    def send_numer(b):
+        for k in (2 * b, 2 * b + 1):
+            if k == 15:
+                continue
+            block = piece(sums.at[0], *owners[k])
+            copy = remote(block, parts_in.at[k], part_send.at[k], part_recv.at[k], peers[k])
+            copy.start()
+            numer_parts.append(copy)
+
+    numer_parts = []
+    here = pl.multiple_of(24 * core, 8)
+    there = pl.multiple_of(24 * (1 - core), 8)
+
+    def start_pair():
+        copy = remote(sums.at[1, :, pl.ds(there, 24)], pair_in, pair_send.at[0], pair_recv.at[0], peers[14])
         copy.start()
         return copy
 
-    def start_parts(q):
+    def add_pair():
         def body(x):
-            half[q, x] = sums[q, x, pl.ds(mine, 24), :] + pair_in[q, x]
-
-        loop(body, CX, 4)
+            half[x] = sums[1, x, pl.ds(here, 24), :] + pair_in[x]
+
+        loop(body, CX, 8)
+
+    def start_denom():
         copies = [
-            remote(half.at[q, pl.ds(3 * other, 3)], parts_in.at[q, k], part_send.at[q, k], part_recv.at[q, k], peers[k])
-            for k, other in enumerate(chips)
+            remote(half.at[pl.ds(3 * owners[2 * b][0], 3)], denom_in.at[b], denom_send.at[b], denom_recv.at[b], peers[2 * b])
+            for b in range(7)
         ]
         for copy in copies:
             copy.start()
         return copies
 
-    bulk = {}
-    for c in range(6):
-        wait(edges[c])
-        smooth_inner(c)
-        if c < 4:
-            bulk[c] = start_bulk(c)
-    for c in range(3):
-        wait(bulk[c])
-        smooth_first(c)
-    for k in range(4):
-        wait(halos[0, k])
-        if k == 1:
-            wait(shift)
-        if k < 3:
-            transport(0, k, stage_columns(0, k + 1))
-            halos[0, k + 1] = start_halo(0, k + 1)
-            if k == 0:
-                shift = start_speed(0)
-            if k < 2:
-                bulk[4 + k] = start_bulk(4 + k)
-        else:
-            transport(0, k, lambda x, values: None)
-        if k == 1:
-            weigh(0)
-            wait(bulk[3])
-            smooth_first(3)
-        if k == 2:
-            wait(bulk[4])
-            smooth_first(4)
+    wait(edges[1])
+    smooth_inner(1)
+    bulk[1] = start_bulk(1)
+    halos = {(s, 0): start_halo(s, 0) for s in range(2)}
+    wait(edges[2])
+    smooth_inner(2)
+    bulk[2] = start_bulk(2)
+    wait(bulk[0])
+    smooth_first(0)
+    edges[0] = start_middle()
+    edges[4] = start_edges(4)
+    edges[5] = start_edges(5)
+    wait(edges[3])
+    smooth_inner(3)
+    bulk[3] = start_bulk(3)
+    wait(bulk[1])
+    smooth_first(1)
+    shift = {0: start_speed_cols(0)}
+    wait(edges[0])
+    smooth_inner_last()
+    shift[0] += start_speed_rows(0)
+    wait(edges[4])
+    smooth_inner(4)
+    wait(edges[5])
+    smooth_inner(5)
+    wait(bulk[2])
+    smooth_first(2)
+    wait(halos[0, 0])
+    transport(0, 0, stage_columns(0, 1))
+    halos[0, 1] = start_halo(0, 1)
+    bulk[4] = start_bulk(4)
+    wait(bulk[3])
+    smooth_first(3)
+    shift[1] = start_speed_rows(1)
+    wait(halos[0, 1])
+    transport(0, 1, stage_columns(0, 2))
+    halos[0, 2] = start_halo(0, 2)
+    bulk[5] = start_bulk(5)
+    wait(shift[0])
+    weigh(0)
+    wait(halos[0, 2])
+    transport(0, 2, stage_columns(0, 3))
+    halos[0, 3] = start_halo(0, 3)
+    wait(bulk[4])
+    smooth_first(4)
+    shift[1] += start_speed_cols(1)
+    wait(halos[1, 0])
 
     wait(bulk[5])
     smooth_first(5)
-    wait(halos[1, 0])
     transport(1, 0, stage_columns(1, 1))
     halos[1, 1] = start_halo(1, 1)
-    shift = start_speed(1)
+    wait(shift[1])
+    weigh(1)
+    pair = start_pair()
+    wait(halos[0, 3])
+    transport(0, 3, lambda x, values: None)
     wait(halos[1, 1])
     transport(1, 1, stage_columns(1, 2))
     halos[1, 2] = start_halo(1, 2)
-    wait(shift)
-    weigh(1)
-    pair = start_pair(1)
+    pair.wait()
+    add_pair()
     wait(halos[1, 2])
     transport(1, 2, stage_columns(1, 3))
     halos[1, 3] = start_halo(1, 3)
-    pair.wait()
-    parts = start_parts(1)
+    denom_parts = start_denom()
     wait(halos[1, 3])
 
     def gather_sum(x, values):
@@ -399,35 +500,26 @@
                 weight[0, x, t : t + 8, :] * warped[0, 0, x + 1, p : p + 8, :] + weight[1, x, t : t + 8, :] * value
             )
 
-    transport(1, 3, gather_sum)
-    pair = start_pair(0)
-    wait(parts)
-    pair.wait()
-    wait(start_parts(0))
-
-    own = 3 * chip
+    transport(1, 3, gather_sum, [owners[2 * b][0] for b in range(7)] + [chip])
+    wait(denom_parts)
+    denom = []
     for x in range(3):
-        total = [half[q, own + x] for q in range(2)]
-        for q in range(2):
-            for k in range(7):
-                total[q] = total[q] + parts_in[q, k, x]
-        whole[own + x, pl.ds(mine, 24), :] = total[0] / (1.0 + total[1])
-
-    def piece(other):
-        return whole.at[pl.ds(3 * other, 3), pl.ds(mine, 24)]
-
-    copies = [remote(piece(chip), piece(chip), gather_send.at[k], gather_recv.at[k], peers[k]) for k in range(7)]
-    onward = [remote(piece(chip), piece(chip), gather_send.at[7], gather_recv.at[7], sibling)]
-    for copy in copies + onward:
+        total = half[3 * chip + x]
+        for k in range(7):
+            total = total + denom_in[k, x]
+        denom.append(1.0 + total)
+    wait(numer_parts)
+    for x in range(3):
+        total = sums[0, 3 * chip + x, pl.ds(here, 24), :]
+        for k in range(15):
+            total = total + parts_in[k, x]
+        whole[3 * chip + x, pl.ds(here, 24), :] = total / denom[x]
+
+    own = piece(whole, chip, core)
+    copies = [remote(own, own, gather_send.at[k], gather_recv.at[k], peers[k]) for k in range(15)]
+    for copy in copies:
         copy.start()
-    for k in range(7):
-        copies[k].wait_recv()
-        block = piece((chip + 7 - k) % 8)
-        onward.append(remote(block, block, gather_send.at[8 + k], gather_recv.at[8 + k], sibling))
-        onward[-1].start()
-    for copy in copies:
-        copy.wait_send()
-    wait(onward)
+    wait(copies)
 
     def finish(x):
         value = whole[x]
@@ -435,7 +527,7 @@
         for s in range(2):
             mismatch_ref[s, x] = (warped[s, 0, x + 1, OWN, :] - value).astype(jnp.bfloat16)
 
-    loop(finish, CX, 4)
+    loop(finish, CX, 8)
 
 
 def build(index, wide):
@@ -447,12 +539,15 @@
             jax.ShapeDtypeStruct((2, CX, CY, CZ), jnp.bfloat16),
             jax.ShapeDtypeStruct((CX, CY, CZ), f32),
         ),
-        in_specs=[pl.BlockSpec(memory_space=pltpu.SMEM)] * 2 + [pl.BlockSpec(memory_space=pltpu.VMEM)] * 2,
+        in_specs=[pl.BlockSpec(memory_space=pltpu.SMEM)] * 2 + [pl.BlockSpec(memory_space=pl.ANY)] * 2,
         out_specs=(pl.BlockSpec(memory_space=pltpu.VMEM),) * 2,
         scratch_shapes=[
+            pltpu.VMEM((2, CX, CY, CZ), jnp.bfloat16),
+            pltpu.VMEM((6, CX, CY, CZ), jnp.bfloat16),
             pltpu.VMEM((6, 2, CX, EDGE, CZ), f32),
             pltpu.VMEM((6, 2, CX, EDGE, CZ), f32),
             pltpu.VMEM((6, CX + 2 * wide, CY, CZ), f32),
+            pltpu.VMEM((CX, CY, CZ), f32),
             pltpu.VMEM((6, CX + 2, CY + 2 * PAD, CZ), f32),
             pltpu.VMEM((2, 2, CX + 2, CY + 2 * PAD, CZ), f32),
             pltpu.VMEM((2, 4, 2, CY, CZ), f32),
@@ -463,10 +558,12 @@
             pltpu.VMEM((2, 2, CX, CZ), f32),
             pltpu.VMEM((2, CX, CY, CZ), f32),
             pltpu.VMEM((2, CX, CY, CZ), f32),
-            pltpu.VMEM((2, CX, 24, CZ), f32),
-            pltpu.VMEM((2, CX, 24, CZ), f32),
-            pltpu.VMEM((2, 7, 3, 24, CZ), f32),
+            pltpu.VMEM((CX, 24, CZ), f32),
+            pltpu.VMEM((CX, 24, CZ), f32),
+            pltpu.VMEM((15, 3, 24, CZ), f32),
+            pltpu.VMEM((7, 3, 24, CZ), f32),
             pltpu.VMEM((CX, CY, CZ), f32),
+            dma((7,)),
             dma((6, 2)),
             dma((6, 2)),
             dma((6, 2)),
@@ -475,10 +572,12 @@
             dma((2, 4, 4)),
             dma((2, 4)),
             dma((2, 4)),
-            dma((2,)),
-            dma((2,)),
-            dma((2, 7)),
-            dma((2, 7)),
+            dma((1,)),
+            dma((1,)),
+            dma((15,)),
+            dma((15,)),
+            dma((7,)),
+            dma((7,)),
             dma((15,)),
             dma((15,)),
         ],

time: 129 us -> 138 us (1.070)
  loops' own time: 0.03 us -> 5.3 us
  Pallas kernels: 126 us -> 130 us
    another operation x1, loops' own time: 0.03 us -> 5.3 us  [per_device(): lax.switch(which, [build(i, 8 + 2 * i) for i in range(3)], *args)]
    pallas_call x1, Pallas kernels: 126 us -> 130 us  [per_device(): lax.switch(which, [build(i, 8 + 2 * i) for i in range(3)], *args)]
where the time goes in v2:
time: 138 us
  Pallas kernels  130 us (94%)
  loops' own time  5.3 us (4%)
  local copies, waits for them, and re-layouts  1.63 us (1%)
    pallas_call x1, Pallas kernels, per_device(): lax.switch(which, [build(i, 8 + 2 * i) for i in range(3)], *args)  130 us
    another operation x1, loops' own time, per_device(): lax.switch(which, [build(i, 8 + 2 * i) for i in range(3)], *args)  5.3 us

profile of v2, /device:TPU:1, one launch (start us, length us, event | category | flops | bytes accessed | tf_op | source)
XLA Modules:
  0.0 138.1 jit_solution(5216727810001384608)
XLA Ops:
  1.3 135.2 %conditional.1 = ((bf16[2,24,48,128]{3,2,1,0:T(8,128)(2,1)S(1)}, f32[24,48,128]{2,1,0:T(8,128)S(1)})) conditional(s32[]{:T(128)} %clamp.3, (s32[3]{0:T(128)}, s32[2]{0:T(128)}, bf16[2,24,48,128]{3,2,1,0:T(8,128)(2,1)}, bf16[6,24,48,128]{3,2,1,0:T(8,128)(2,1)}) %tuple.44, (s32[3]{0:T(128)}, s32[2]{0:T(128)}, ...), branch_computations={%region_0.1_spmd, %region_1.2_spmd, %region_2.3_spmd} | conditional | bytes 8 | solution.py:598
  6.4 129.9 %branch_2_fun.1 = (bf16[2,24,48,128]{3,2,1,0:T(8,128)(2,1)S(1)}, f32[24,48,128]{2,1,0:T(8,128)S(1)}) custom-call(s32[3]{0:T(128)} %get-tuple-element.44.widths_ref, s32[2]{0:T(128)} %get-tuple-element.45.flags_ref, bf16[2,24,48,128]{3,2,1,0:T(8,128)(2,1)} %get-tuple-element.46.image_hbm, bf16[6,24,48,128]{3,2,1,0:T(8,128)(2,1)} %get-tuple-element.47.moment_hbm), custom_call_target="tpu_custom_call" | custom-call | tf_op jit(solution)/shard_map/cond/branch_2_fun/pallas_call | solution.py:598
  136.5 0.8 copy.14
  137.3 0.8 copy.15

commit v3 on v2

--- a/solution.py
+++ b/solution.py
@@ -147,11 +147,18 @@
             copy.start()
         return pair
 
-    def start_halo(s, k):
+    def start_rows(s, k):
         slot = k % 2
         copies = (
             remote(warped.at[s, slot, 1, OWN], rows_in.at[s, k, 1], step_send.at[s, k, N], step_recv.at[s, k, N], place[N]),
             remote(warped.at[s, slot, CX, OWN], rows_in.at[s, k, 0], step_send.at[s, k, S], step_recv.at[s, k, S], place[S]),
+        )
+        for copy in copies:
+            copy.start()
+        return copies
+
+    def start_cols(s, k):
+        copies = (
             remote(cols_out.at[s, k, 0], cols_in.at[s, k, 1], step_send.at[s, k, W], step_recv.at[s, k, W], place[W]),
             remote(cols_out.at[s, k, 1], cols_in.at[s, k, 0], step_send.at[s, k, E], step_recv.at[s, k, E], place[E]),
         )
@@ -225,7 +232,7 @@
     scale = jnp.full((8, CZ), 1.0 / STEPS, jnp.float32) / jnp.full((8, CZ), 1.0, jnp.float32) / norm
 
     def smooth_inner(c):
-        group = 12
+        group = 12 if c == 1 else 4
 
         def body(g):
             blocks = []
@@ -256,7 +263,7 @@
         return high, (value - high.astype(jnp.float32)).astype(jnp.bfloat16)
 
     def smooth_inner_last():
-        group = 12
+        group = 4
 
         def body(g):
             blocks = []
@@ -349,7 +356,13 @@
                 values.append(value)
             after(x, values)
 
-        if blocks is None:
+        if blocks is None and k < 3:
+            body(0)
+            body(CX - 1)
+            copies = start_rows(s, k + 1)
+            loop(lambda x: body(x + 1), CX - 2, 2 if s == 0 and k < 2 else 11)
+            halos[s, k + 1] = copies + start_cols(s, k + 1)
+        elif blocks is None:
             loop(body, CX, 8)
         else:
             for b, block in enumerate(blocks):
@@ -426,10 +439,12 @@
             copy.start()
         return copies
 
+    halos = {}
     wait(edges[1])
     smooth_inner(1)
     bulk[1] = start_bulk(1)
-    halos = {(s, 0): start_halo(s, 0) for s in range(2)}
+    for s in range(2):
+        halos[s, 0] = start_rows(s, 0) + start_cols(s, 0)
     wait(edges[2])
     smooth_inner(2)
     bulk[2] = start_bulk(2)
@@ -449,26 +464,21 @@
     shift[0] += start_speed_rows(0)
     wait(edges[4])
     smooth_inner(4)
+    bulk[4] = start_bulk(4)
     wait(edges[5])
     smooth_inner(5)
     wait(bulk[2])
     smooth_first(2)
     wait(halos[0, 0])
     transport(0, 0, stage_columns(0, 1))
-    halos[0, 1] = start_halo(0, 1)
-    bulk[4] = start_bulk(4)
+    bulk[5] = start_bulk(5)
     wait(bulk[3])
     smooth_first(3)
     shift[1] = start_speed_rows(1)
+    wait(shift[0])
+    weigh(0)
     wait(halos[0, 1])
     transport(0, 1, stage_columns(0, 2))
-    halos[0, 2] = start_halo(0, 2)
-    bulk[5] = start_bulk(5)
-    wait(shift[0])
-    weigh(0)
-    wait(halos[0, 2])
-    transport(0, 2, stage_columns(0, 3))
-    halos[0, 3] = start_halo(0, 3)
     wait(bulk[4])
     smooth_first(4)
     shift[1] += start_speed_cols(1)
@@ -477,20 +487,19 @@
     wait(bulk[5])
     smooth_first(5)
     transport(1, 0, stage_columns(1, 1))
-    halos[1, 1] = start_halo(1, 1)
+    wait(halos[0, 2])
+    transport(0, 2, stage_columns(0, 3))
     wait(shift[1])
     weigh(1)
     pair = start_pair()
+    wait(halos[1, 1])
+    transport(1, 1, stage_columns(1, 2))
     wait(halos[0, 3])
     transport(0, 3, lambda x, values: None)
-    wait(halos[1, 1])
-    transport(1, 1, stage_columns(1, 2))
-    halos[1, 2] = start_halo(1, 2)
     pair.wait()
     add_pair()
     wait(halos[1, 2])
     transport(1, 2, stage_columns(1, 3))
-    halos[1, 3] = start_halo(1, 3)
     denom_parts = start_denom()
     wait(halos[1, 3])
 
@@ -516,10 +525,18 @@
         whole[3 * chip + x, pl.ds(here, 24), :] = total / denom[x]
 
     own = piece(whole, chip, core)
-    copies = [remote(own, own, gather_send.at[k], gather_recv.at[k], peers[k]) for k in range(15)]
-    for copy in copies:
+    across = [remote(own, own, gather_send.at[b], gather_recv.at[b], peers[2 * b]) for b in range(7)]
+    onward = [remote(own, own, gather_send.at[7], gather_recv.at[7], peers[14])]
+    for copy in across + onward:
         copy.start()
-    wait(copies)
+    for b in range(7):
+        across[b].wait_recv()
+        block = piece(whole, (chip + 7 - b) % 8, core)
+        onward.append(remote(block, block, gather_send.at[8 + b], gather_recv.at[8 + b], peers[14]))
+        onward[-1].start()
+    for copy in across:
+        copy.wait_send()
+    wait(onward)
 
     def finish(x):
         value = whole[x]

time: 138 us -> 103 us (0.75)
  Pallas kernels: 130 us -> 99.5 us
  loops' own time: 5.3 us -> 0.24 us
    pallas_call x1, Pallas kernels: 130 us -> 99.5 us  [per_device(): lax.switch(which, [build(i, 8 + 2 * i) for i in range(3)], *args)]
    another operation x1, loops' own time: 5.3 us -> 0.24 us  [per_device(): lax.switch(which, [build(i, 8 + 2 * i) for i in range(3)], *args)]
where the time goes in v3:
time: 103 us
  Pallas kernels  99.5 us (97%)
  local copies, waits for them, and re-layouts  1.63 us (2%)
  between operations  1.31 us (1%)
    pallas_call x1, Pallas kernels, per_device(): lax.switch(which, [build(i, 8 + 2 * i) for i in range(3)], *args)  99.5 us

profile of v3, /device:TPU:1, one launch (start us, length us, event | category | flops | bytes accessed | tf_op | source)
XLA Modules:
  0.0 102.7 jit_solution(7550829357990074457)
XLA Ops:
  1.3 99.8 %conditional.1 = ((bf16[2,24,48,128]{3,2,1,0:T(8,128)(2,1)S(1)}, f32[24,48,128]{2,1,0:T(8,128)S(1)})) conditional(s32[]{:T(128)} %clamp.3, (s32[3]{0:T(128)}, s32[2]{0:T(128)}, bf16[2,24,48,128]{3,2,1,0:T(8,128)(2,1)}, bf16[6,24,48,128]{3,2,1,0:T(8,128)(2,1)}) %tuple.44, (s32[3]{0:T(128)}, s32[2]{0:T(128)}, ...), branch_computations={%region_0.1_spmd, %region_1.2_spmd, %region_2.3_spmd} | conditional | bytes 8 | solution.py:615
  1.3 99.5 %branch_0_fun.1 = (bf16[2,24,48,128]{3,2,1,0:T(8,128)(2,1)S(1)}, f32[24,48,128]{2,1,0:T(8,128)S(1)}) custom-call(s32[3]{0:T(128)} %get-tuple-element.32.widths_ref, s32[2]{0:T(128)} %get-tuple-element.33.flags_ref, bf16[2,24,48,128]{3,2,1,0:T(8,128)(2,1)} %get-tuple-element.34.image_hbm, bf16[6,24,48,128]{3,2,1,0:T(8,128)(2,1)} %get-tuple-element.35.moment_hbm), custom_call_target="tpu_custom_call" | custom-call | tf_op jit(solution)/shard_map/cond/branch_0_fun/pallas_call | solution.py:615
  101.1 0.8 copy.14
  101.9 0.8 copy.15
